TPU v7x, 256 devices: a whole 4x4x8 slice. The times are simulated.
256 devices in a mesh: grp: 8 (over x, core), dev: 32 (over y, z).
Axes of the slice: x: 4, y: 4, z: 8, core: 2. Of those that a mesh axis runs over, the one named last changes fastest.
Arguments:
- q_latent: bfloat16 [4096, 1536], P(('grp', 'dev')), parts along dimension 0, may hold values from -51 to 51
- w_uq: bfloat16 [1536, 12288], P(None, 'dev'), may hold values from -0.15625 to 0.15625
- w_kup: bfloat16 [8192, 512], P('dev'), may hold values from -0.25 to 0.25
- w_vup: bfloat16 [512, 8192], P(None, 'dev'), may hold values from -0.25 to 0.25
- prefix_keys: bfloat16 [32768, 8192], P('grp', 'dev'), parts along dimension 0, may hold values from -6 to 6
- prefix_values: bfloat16 [32768, 8192], P('grp', 'dev'), parts along dimension 0, may hold values from -6 to 6
- prefix_rope: bfloat16 [64, 32768], P(None, 'grp'), parts along dimension 1, may hold values from -6 to 6
- private_cache: bfloat16 [4096, 384, 576], P(('grp', 'dev')), parts along dimension 0, may hold values from -6 to 6
- lengths: int32 [4096], P(('grp', 'dev')), parts along dimension 0, may hold values from 1 to 384, 98304 in all
- prefix_len: int32 [8], P('grp'), parts along dimension 0, may hold values from 2048 to 4096
Outputs:
- attn: bfloat16 [4096, 8192], P('grp', 'dev'), parts along dimension 0
There are 8 independent parts, one for each index of `grp`. A program takes and returns all parts, laid end to end along the dimension named above; an argument that names none is the same for every part. Nothing has to cross between parts.
Inputs may be any that keep to these rules, and one draw needn't show every extreme that they name: Within each group the lengths sum to 98304.
All inputs are finite; a program needn't handle non-finite values.
Results may differ from a plain program's by a relative error of at most 0.04.
Values may be sent and summed in bfloat16 or wider, within the bound.
A program may use at most 128 MiB of HBM per device.

v0:
```python
import math

import jax
import jax.numpy as jnp
from jax import lax
from jax.sharding import PartitionSpec as P

KVL = 512
NOPE = 128
ROPE = 64
VD = 128


def body(
    q_latent,
    w_uq,
    w_kup,
    w_vup,
    prefix_keys,
    prefix_values,
    prefix_rope,
    private_cache,
    lengths,
    prefix_len,
):
    n_dev = lax.axis_size("dev")
    head_dev = w_kup.shape[0] // NOPE
    req_dev = q_latent.shape[0]
    slots = private_cache.shape[1]
    prefix_slots = prefix_keys.shape[0]
    scale = 1.0 / math.sqrt(NOPE + ROPE)
    q_full = jnp.dot(
        lax.all_gather(q_latent, "dev", axis=0, tiled=True),
        w_uq,
        preferred_element_type=jnp.float32,
    ).astype(jnp.bfloat16)
    total = q_full.shape[0]
    q_full = q_full.reshape(total, head_dev, NOPE + ROPE)
    q_nope = q_full[:, :, :NOPE]
    q_rope = q_full[:, :, NOPE:]
    kup_heads = w_kup.reshape(head_dev, NOPE, KVL)
    absorbed = jnp.einsum(
        "rhn,hnc->hrc", q_nope, kup_heads, preferred_element_type=jnp.float32
    ).astype(jnp.bfloat16)
    q_abs = jnp.concatenate([absorbed, jnp.transpose(q_rope, (1, 0, 2))], axis=2)
    blocks = q_abs.reshape(head_dev, n_dev, req_dev, KVL + ROPE)
    halves = 1
    part_rows = req_dev // halves
    sent = blocks.reshape(head_dev, n_dev * part_rows, KVL + ROPE)
    queries = lax.all_to_all(sent, "dev", split_axis=1, concat_axis=0, tiled=True)
    scores = (
        jnp.einsum("hrc,rjc->hrj", queries, private_cache, preferred_element_type=jnp.float32)
        * scale
    )
    mask = jnp.arange(slots)[None, None, :] < lengths[None, :, None]
    scores = jnp.where(mask, scores, -jnp.inf)
    top = jnp.max(scores, axis=2, keepdims=True)
    expo = jnp.exp(scores - top)
    denom = jnp.sum(expo, axis=2)
    weights = expo.astype(jnp.bfloat16)
    latent = jnp.einsum(
        "hrj,rjc->hrc", weights, private_cache[:, :, :KVL], preferred_element_type=jnp.float32
    )
    latent = (latent / denom[:, :, None]).astype(jnp.bfloat16)
    lse_here = top[:, :, 0] + jnp.log(denom)
    back = lax.all_to_all(latent, "dev", split_axis=0, concat_axis=1, tiled=True)
    back_lse = lax.all_to_all(
        lse_here.astype(jnp.bfloat16), "dev", split_axis=0, concat_axis=1, tiled=True
    ).astype(lse_here.dtype)
    returned = back.reshape(head_dev, n_dev, part_rows, back.shape[2])
    returned_lse = back_lse.reshape(head_dev, n_dev, part_rows)
    gathered_back = returned.reshape(head_dev, total, -1)
    private_lse = returned_lse.reshape(head_dev, total)
    vup_heads = w_vup.reshape(KVL, head_dev, VD)
    private_out = jnp.einsum(
        "hrc,chv->hrv", gathered_back, vup_heads, preferred_element_type=jnp.float32
    )
    key_heads = prefix_keys.reshape(prefix_slots, head_dev, NOPE)
    value_heads = prefix_values.reshape(prefix_slots, head_dev, VD)
    prefix_scores = jnp.einsum(
        "rhn,thn->hrt", q_nope, key_heads, preferred_element_type=jnp.float32
    )
    prefix_scores = prefix_scores + jnp.einsum(
        "rhd,dt->hrt", q_rope, prefix_rope, preferred_element_type=jnp.float32
    )
    prefix_scores = prefix_scores * scale
    prefix_mask = jnp.arange(prefix_slots)[None, None, :] < prefix_len[0]
    prefix_scores = jnp.where(prefix_mask, prefix_scores, -jnp.inf)
    prefix_top = jnp.max(prefix_scores, axis=2, keepdims=True)
    prefix_exp = jnp.exp(prefix_scores - prefix_top)
    prefix_den = jnp.sum(prefix_exp, axis=2)
    prefix_weights = prefix_exp.astype(jnp.bfloat16)
    prefix_out = jnp.einsum(
        "hrt,thv->hrv", prefix_weights, value_heads, preferred_element_type=jnp.float32
    )
    prefix_out = prefix_out / prefix_den[:, :, None]
    prefix_lse = prefix_top[:, :, 0] + jnp.log(prefix_den)
    upper = jnp.maximum(prefix_lse, private_lse)
    first = jnp.exp(prefix_lse - upper)[:, :, None]
    second = jnp.exp(private_lse - upper)[:, :, None]
    merged = (first * prefix_out + second * private_out) / (first + second)
    return jnp.transpose(merged, (1, 0, 2)).reshape(total, head_dev * VD).astype(jnp.bfloat16)


def solution(mesh):
    placed = (
        P(("grp", "dev"), None),
        P(None, "dev"),
        P("dev", None),
        P(None, "dev"),
        P("grp", "dev"),
        P("grp", "dev"),
        P(None, "grp"),
        P(("grp", "dev"), None, None),
        P(("grp", "dev")),
        P("grp"),
    )
    return jax.shard_map(
        body, mesh=mesh, in_specs=placed, out_specs=P("grp", "dev"), check_vma=False
    )
```

profile of v0, /device:TPU:6, one launch (start us, length us, event | category | flops | bytes accessed | tf_op | source)
XLA Modules:
  0.0 198.0 jit_solution(5671329530296933510)
XLA Ops:
  6.5 0.0 copy-start
  6.5 0.0 all-gather.2.cloned.1.call-start
  6.5 0.7 all-gather.2.cloned.1.call-update
  7.9 0.0 copy-start.7
  7.9 82.2 %all-gather.2.cloned.1.call-done = bf16[512,1536]{1,0:T(8,128)(2,1)} async-done(((bf16[16,1536]{1,0:T(8,128)(2,1)}), bf16[512,1536]{1,0:T(8,128)(2,1)}) %all-gather.2.cloned.1.call-update) | async-done | bytes 1572880 | tf_op jit(solution)/shard_map/all_gather | solution.py:33
  90.2 2.6 %convolution_convert_fusion.1 = bf16[512,384]{0,1:T(8,128)(2,1)S(1)} fusion(bf16[512,1536]{1,0:T(8,128)(2,1)} %all-gather.2.cloned.1.call-done, bf16[1536,384]{1,0:T(8,128)(2,1)} %param.11), kind=kOutput, calls=%fused_computation.21 | convolution fusion | flops 604176384 | bytes 3145728 | tf_op jit(solution)/shard_map/dot_general | solution.py:32
  92.7 0.0 copy-start.3
  92.8 0.7 copy-done.3
  93.5 0.0 copy-done.7
  93.5 0.5 convolution_convert_fusion
  94.0 0.1 pad_maximum_fusion
  94.0 2.8 %copy.37 = bf16[2,512,576]{2,0,1:T(2,128)(2,1)} copy(bf16[2,512,576]{1,2,0:T(8,128)(2,1)S(1)} %pad_maximum_fusion) | data formatting | bytes 2359296 | tf_op jit(solution)/shard_map/concatenate | solution.py:45
  96.9 5.9 %all-to-all-start = ((bf16[2,512,576]{2,0,1:T(2,128)(2,1)}), bf16[2,512,576]{2,0,1:T(2,128)(2,1)S(1)}, u32[]{:S(2)}, u32[]{:S(2)}) async-start(bf16[2,512,576]{2,0,1:T(2,128)(2,1)} %copy.37), calls=%async_computation | async-start | bytes 2621440 | tf_op jit(solution)/shard_map/all_to_all | solution.py:50
  102.8 1.8 copy.50
  104.6 0.0 copy-start.8
  104.6 4.1 %copy.49 = bf16[4096,256]{0,1:T(8,128)(2,1)} copy(bf16[4096,256]{1,0:T(8,128)(2,1)} %param.15) | data formatting | bytes 4194304 | tf_op jit(solution)/shard_map/reshape | solution.py:79
  108.7 0.0 copy-done.8
  108.7 0.1 iota_compare_fusion
  108.8 0.0 copy-start.4
  108.8 9.3 %fusion.32 = f32[512,2,4096]{2,0,1:T(8,128)} fusion(bf16[64,4096]{1,0:T(8,128)(2,1)} %param.16, bf16[512,2,192]{0,2,1:T(8,128)(2,1)} %bitcast.87), kind=kOutput, calls=%fused_computation.32 | convolution fusion | flops 536870912 | bytes 17432576 | tf_op jit(solution)/shard_map/rhd,dt->hrt/dot_general | solution.py:83
  118.1 0.0 copy-done
  118.1 0.0 copy-done.4
  118.1 10.9 %fusion.41 = (f32[2,512]{1,0:T(2,128)S(1)}, f32[2,512,4096]{2,1,0:T(8,128)}) fusion(f32[512,2,4096]{2,0,1:T(8,128)} %fusion.32, bf16[512,2,192]{0,2,1:T(8,128)(2,1)S(1)} %bitcast.88, pred[4096]{0:T(1024)(128)(4,1)S(1)} %iota_compare_fusion.1, bf16[4096,256]{1,0:T(8,128)(2,1)S(1)} %copy-done), kind=kOutput, calls=%fused_computation.48 | convolution fusion | flops 1090518016 | bytes 35921920 | tf_op jit(solution)/shard_map/rhn,thn->hrt/dot_general | solution.py:80
  128.9 3.4 %all-to-all-done = bf16[2,512,576]{2,0,1:T(2,128)(2,1)S(1)} async-done(((bf16[2,512,576]{2,0,1:T(2,128)(2,1)}), bf16[2,512,576]{2,0,1:T(2,128)(2,1)S(1)}, u32[]{:S(2)}, u32[]{:S(2)}) %all-to-all-start) | async-done | bytes 1179680 | tf_op jit(solution)/shard_map/all_to_all | solution.py:50
  132.4 0.2 copy.38
  132.5 2.4 %copy.39 = bf16[32,2,16,576]{3,1,0,2:T(2,128)(2,1)} copy(bf16[32,2,16,576]{3,2,0,1:T(8,128)(2,1)S(1)} %bitcast.83) | data formatting | bytes 2359296 | tf_op jit(solution)/shard_map/all_to_all | solution.py:50
  135.0 3.2 %all_to_all.37 = bf16[64,16,576]{2,0,1:T(8,128)(2,1)S(1)} reshape(bf16[32,2,16,576]{3,1,0,2:T(2,128)(2,1)} %copy.39) | data formatting | bytes 2359296 | tf_op jit(solution)/shard_map/all_to_all | solution.py:50
  138.1 4.5 %bitcast_reduce_fusion = (f32[64,16]{0,1:T(8,128)S(1)}, f32[16,64,384]{2,1,0:T(8,128)S(1)}) fusion(bf16[64,16,576]{2,0,1:T(8,128)(2,1)S(1)} %all_to_all.37, bf16[16,384,576]{1,2,0:T(8,128)(2,1)} %param.17, pred[16,384]{1,0:T(8,128)(4,1)S(1)} %iota_compare_fusion), kind=kOutput, calls=%fused_computation.15 | convolution fusion | flops 454163456 | bytes 9840640 | tf_op jit(solution)/shard_map/hrc,rjc->hrj/dot_general | solution.py:52
  142.7 0.6 fusion.16
  143.3 0.7 copy.40
  144.0 6.5 %all-to-all-start.1 = ((bf16[32,2,16]{2,1,0:T(2,128)(2,1)}), bf16[32,2,16]{2,1,0:T(2,128)(2,1)S(1)}, u32[]{:S(2)}, u32[]{:S(2)}) async-start(bf16[32,2,16]{2,1,0:T(2,128)(2,1)} %bitcast.9), calls=%async_computation.1 | async-start | bytes 32768 | tf_op jit(solution)/shard_map/all_to_all | solution.py:67
  150.5 4.9 %fusion.11 = bf16[64,16,512]{2,0,1:T(8,128)(2,1)S(1)} fusion(bf16[16,384,576]{1,2,0:T(8,128)(2,1)} %param.17, f32[64,16]{0,1:T(8,128)S(1)} %fusion.16, f32[16,64,384]{2,1,0:T(8,128)S(1)} %get-tuple-element.11, f32[64,16]{0,1:T(8,128)S(1)} %get-tuple-element.10), kind=kOutput, calls=%fused_computation.13 | convolution fusion | flops 404488192 | bytes 8921088 | tf_op jit(solution)/shard_map/hrj,rjc->hrc/dot_general | solution.py:61
  155.4 1.6 copy.44
  157.0 3.1 %all-to-all-done.1 = bf16[32,2,16]{2,1,0:T(2,128)(2,1)S(1)} async-done(((bf16[32,2,16]{2,1,0:T(2,128)(2,1)}), bf16[32,2,16]{2,1,0:T(2,128)(2,1)S(1)}, u32[]{:S(2)}, u32[]{:S(2)}) %all-to-all-start.1) | async-done | bytes 2080 | tf_op jit(solution)/shard_map/all_to_all | solution.py:67
  160.1 6.5 %all-to-all-start.2 = ((bf16[64,16,512]{2,1,0:T(8,128)(2,1)}), bf16[64,16,512]{2,1,0:T(8,128)(2,1)S(1)}, u32[]{:S(2)}, u32[]{:S(2)}) async-start(bf16[64,16,512]{2,1,0:T(8,128)(2,1)} %copy.44), calls=%async_computation.2 | async-start | bytes 2097152 | tf_op jit(solution)/shard_map/all_to_all | solution.py:66
  166.6 0.0 copy-start.2
  166.6 8.2 %fusion.3 = f32[2,512]{1,0:T(2,128)S(1)} fusion(f32[2,512,4096]{2,1,0:T(8,128)} %get-tuple-element.9, f32[2,512]{1,0:T(2,128)S(1)} %get-tuple-element.8), kind=kLoop, calls=%fused_computation.5 | loop fusion | flops 8387584 | bytes 16785408 | tf_op jit(solution)/shard_map/reduce_sum | solution.py:91
  174.9 0.1 reshape.95
  175.0 0.0 copy-done.2
  175.0 9.6 %fusion.27 = f32[512,2,128]{0,2,1:T(8,128)} fusion(bf16[4096,2,128]{0,2,1:T(8,128)(2,1)S(1)} %bitcast.82, f32[2,512,4096]{2,1,0:T(8,128)} %get-tuple-element.9, f32[2,512]{1,0:T(2,128)S(1)} %get-tuple-element.8, f32[512,2]{0,1:T(2,128)S(1)} %bitcast.93, f32[512,2]{0,1:T(2,128)S(1)} %bitcast.94), kind=kOutput, calls=%fused_computation.30 | convolution fusion | flops 1082392576 | bytes 19410944 | tf_op jit(solution)/shard_map/hrt,thv->hrv/dot_general | solution.py:93
  184.6 0.0 copy-start.6
  184.6 4.2 %all-to-all-done.2 = bf16[64,16,512]{2,1,0:T(8,128)(2,1)S(1)} async-done(((bf16[64,16,512]{2,1,0:T(8,128)(2,1)}), bf16[64,16,512]{2,1,0:T(8,128)(2,1)S(1)}, u32[]{:S(2)}, u32[]{:S(2)}) %all-to-all-start.2) | async-done | bytes 1048608 | tf_op jit(solution)/shard_map/all_to_all | solution.py:66
  188.8 0.0 copy-start.5
  188.8 0.0 copy-start.1
  188.8 0.1 copy.45
  188.9 0.0 copy-done.6
  188.9 0.9 copy-done.5
  189.9 0.5 fusion.23
  190.4 0.8 copy.47
  191.2 0.0 copy-done.1
  (6 shorter events, 0.1 us)
Async XLA Ops:
  6.5 111.5 %copy-start = (bf16[4096,256]{1,0:T(8,128)(2,1)S(1)}, bf16[4096,256]{1,0:T(8,128)(2,1)}, u32[]{:S(2)}) copy-start(bf16[4096,256]{1,0:T(8,128)(2,1)} %param.14) | copy-start | bytes 6291460
  6.5 83.6 %all-gather.2.cloned.1.call-start = ((), (), s32[]{:S(2)}) async-start(), calls=%async_computation.3 | async-start | bytes 1622016 | tf_op jit(solution)/shard_map/all_gather | solution.py:33
  7.9 85.6 %copy-start.7 = (bf16[256,512]{1,0:T(8,128)(2,1)S(1)}, bf16[256,512]{1,0:T(8,128)(2,1)}, u32[]{:S(2)}) copy-start(bf16[256,512]{1,0:T(8,128)(2,1)} %param.12) | copy-start | bytes 786436
  92.7 0.7 copy-start.3
  96.9 35.5 %all-to-all-start = ((bf16[2,512,576]{2,0,1:T(2,128)(2,1)}), bf16[2,512,576]{2,0,1:T(2,128)(2,1)S(1)}, u32[]{:S(2)}, u32[]{:S(2)}) async-start(bf16[2,512,576]{2,0,1:T(2,128)(2,1)} %copy.37), calls=%async_computation | async-start | bytes 2621440 | tf_op jit(solution)/shard_map/all_to_all | solution.py:50
  104.6 4.1 %copy-start.8 = (s32[16]{0:T(128)S(1)}, s32[16]{0:T(128)}, u32[]{:S(2)}) copy-start(s32[16]{0:T(128)} %param.18) | copy-start | bytes 196
  108.8 9.3 %copy-start.4 = (bf16[512,384]{0,1:T(8,128)(2,1)S(1)}, bf16[512,384]{0,1:T(8,128)(2,1)}, u32[]{:S(2)}) copy-start(bf16[512,384]{0,1:T(8,128)(2,1)} %copy-done.3) | copy-start | bytes 1179652
  144.0 16.1 %all-to-all-start.1 = ((bf16[32,2,16]{2,1,0:T(2,128)(2,1)}), bf16[32,2,16]{2,1,0:T(2,128)(2,1)S(1)}, u32[]{:S(2)}, u32[]{:S(2)}) async-start(bf16[32,2,16]{2,1,0:T(2,128)(2,1)} %bitcast.9), calls=%async_computation.1 | async-start | bytes 32768 | tf_op jit(solution)/shard_map/all_to_all | solution.py:67
  160.1 28.7 %all-to-all-start.2 = ((bf16[64,16,512]{2,1,0:T(8,128)(2,1)}), bf16[64,16,512]{2,1,0:T(8,128)(2,1)S(1)}, u32[]{:S(2)}, u32[]{:S(2)}) async-start(bf16[64,16,512]{2,1,0:T(8,128)(2,1)} %copy.44), calls=%async_computation.2 | async-start | bytes 2097152 | tf_op jit(solution)/shard_map/all_to_all | solution.py:66
  166.6 8.4 %copy-start.2 = (bf16[4096,256]{0,1:T(8,128)(2,1)S(1)}, bf16[4096,256]{0,1:T(8,128)(2,1)}, u32[]{:S(2)}) copy-start(bf16[4096,256]{0,1:T(8,128)(2,1)} %copy.49) | copy-start | bytes 6291460
  184.6 4.3 %copy-start.6 = (bf16[512,256]{0,1:T(8,128)(2,1)S(1)}, bf16[512,256]{0,1:T(8,128)(2,1)}, u32[]{:S(2)}) copy-start(bf16[512,256]{0,1:T(8,128)(2,1)} %copy.50) | copy-start | bytes 786436
  188.8 1.0 copy-start.5
  188.8 2.4 %copy-start.1 = (bf16[4096,256]{1,0:T(8,128)(2,1)S(1)}, bf16[4096,256]{1,0:T(8,128)(2,1)}, u32[]{:S(2)}) copy-start(bf16[4096,256]{1,0:T(8,128)(2,1)} %param.14) | copy-start | bytes 6291460
Sparse Core Ops, SparseCore 0:
  9.9 80.1 all-gather.1
where the time goes:
time: 199 us; the launch traced here: 198 us
  waiting for transfers between devices  93.7 us (47%)
  matrix products  42.7 us (21%)
  local copies, waits for them, and re-layouts  19.4 us (10%)
  starting transfers between devices  19 us (10%)
  between operations  14.2 us (7%)
  other arithmetic  9.01 us (5%)
    all_gather x1, waiting for transfers between devices, body(): lax.all_gather(q_latent, 'dev', axis=0, tiled=True)  82.2 us
    dot_general x1, matrix products, body(): jnp.einsum('rhn,thn->hrt', q_nope, key_heads, preferred_element_type=jnp....  10.9 us
    dot_general x1, matrix products, body(): jnp.einsum('hrt,thv->hrv', prefix_weights, value_heads, preferred_element...  9.59 us
    dot_general x1, matrix products, body(): jnp.einsum('rhd,dt->hrt', q_rope, prefix_rope, preferred_element_type=jnp...  9.27 us
    reduce_sum x1, other arithmetic, body(): prefix_den = jnp.sum(prefix_exp, axis=2)  8.25 us
    all_to_all x1, starting transfers between devices, body(): lax.all_to_all(lse_here.astype(jnp.bfloat16), 'dev', split_axis=0, concat...  6.54 us
    all_to_all x1, starting transfers between devices, body(): lax.all_to_all(latent, 'dev', split_axis=0, concat_axis=1, tiled=True)  6.5 us
    all_to_all x1, starting transfers between devices, body(): lax.all_to_all(sent, 'dev', split_axis=1, concat_axis=0, tiled=True)  5.93 us
  transfers between devices with their start and end apart: 4, of which 4 were waited for; matrix products, arithmetic and copies ran while one was open for 26% of the time, Pallas kernels for 0%

commit v1 on v0

v1 whole, which is shorter than its diff:
```python
import math

import jax
import jax.numpy as jnp
from jax import lax
from jax.experimental import pallas as pl
from jax.experimental.pallas import tpu as pltpu
from jax.sharding import PartitionSpec as P

KVL = 512
NOPE = 128
ROPE = 64
VD = 128
MESH = pl.DeviceIdType.MESH
NY, NZ, NX = 4, 8, 4
RQ = 16
SLOTS = 384
PREFIX = 4096
QL = 1536
TB = 512
SCALE2 = math.log2(math.e) / math.sqrt(NOPE + ROPE)
F32 = jnp.float32
BF16 = jnp.bfloat16


def nn(a, b):
    return lax.dot_general(a, b, (((1,), (0,)), ((), ())), preferred_element_type=F32)


def nt(a, b):
    return lax.dot_general(a, b, (((1,), (1,)), ((), ())), preferred_element_type=F32)


def near(i):
    odd = lax.rem(i, 2)
    return odd * lax.div(i + 1, 2) + (1 - odd) * (NZ - lax.div(i, 2))


def each(low, high, step):
    def one(i, carry):
        step(i)
        return carry

    lax.fori_loop(low, high, one, 0)


def kernel(
    ql, wuq, wkup, wvup, keys_h, vals_h, rope_h, cache_h, lens, plen, out,
    wuq_v, wp, keys, vals, rope, cache, ag, qb, zq, wk, wv, absb, rps, rec1, rec1r,
    qf, qrf, lf, lse, send2, rec2, recl, outz, mbuf, recz, recm, sc, po, plse,
    ld, agz_s, agz_r, yp_s, yp_r, ym_s, ym_r, f_s, f_r, qz_s, qz_r,
    kz_s, kz_r, kx_s, kx_r, kc_s, kc_r, vz_s, vz_r, vx_s, vx_r, vc_s, vc_r,
    a_s, a_r, ar_s, ar_r, b_s, b_r, bl_s, bl_r, c_s, c_r, cm_s, cm_r,
):
    g = lax.axis_index("grp")
    d = lax.axis_index("dev")
    x, c = lax.div(g, 2), lax.rem(g, 2)
    y, z = lax.div(d, NZ), lax.rem(d, NZ)

    def yat(k):
        return lax.rem(y + (k + NY), NY)

    def zat(k):
        return lax.rem(z + (k + NZ), NZ)

    def to_y(k):
        return (g, yat(k) * NZ + z)

    def to_z(k):
        return (g, y * NZ + zat(k))

    def to_x(k):
        return (lax.rem(x + k, NX) * 2 + c, d)

    twin = (x * 2 + 1 - c, d)
    sends = []

    def copy(src, dst, ss, rs, dev):
        return pltpu.make_async_remote_copy(
            src_ref=src, dst_ref=dst, send_sem=ss, recv_sem=rs, device_id=dev, device_id_type=MESH
        )

    def push(*what):
        one = copy(*what)
        one.start()
        sends.append(one.wait_send)

    def push_near(what):
        each(1, NZ, lambda i: what(near(i)).start())
        sends.append(lambda: each(1, NZ, lambda i: what(i).wait_send()))

    def push_x(what):
        each(1, NX, lambda i: what(i).start())
        sends.append(lambda: each(1, NX, lambda i: what(i).wait_send()))

    def landed(dst, ss, rs):
        pltpu.make_async_remote_copy(
            src_ref=dst, dst_ref=dst, send_sem=ss, recv_sem=rs, device_id=twin, device_id_type=MESH
        ).wait_recv()

    krow = pl.multiple_of(c * 128 + x * 32, 32)
    vrow = pl.multiple_of(x * 128, 128)
    vcol = pl.multiple_of(c * 128, 128)
    ccol = pl.multiple_of((1 - c) * 128, 128)

    loads = [
        pltpu.make_async_copy(ql, ag.at[y, z], ld.at[0]),
        pltpu.make_async_copy(wuq, wuq_v, ld.at[1]),
        pltpu.make_async_copy(wkup.at[pl.ds(krow, 32), :], wk.at[z, pl.ds(krow, 32), :], ld.at[2]),
        pltpu.make_async_copy(
            wvup.at[pl.ds(vrow, 128), pl.ds(vcol, 128)],
            wv.at[z, c, pl.ds(vrow, 128), :],
            ld.at[3],
        ),
        pltpu.make_async_copy(keys_h, keys, ld.at[4]),
        pltpu.make_async_copy(rope_h, rope, ld.at[5]),
        pltpu.make_async_copy(vals_h, vals, ld.at[6]),
        pltpu.make_async_copy(cache_h, cache, ld.at[7]),
    ]
    for load in loads:
        load.start()

    barrier = pltpu.get_barrier_semaphore()

    def greet(dev):
        pl.semaphore_signal(barrier, inc=1, device_id=dev, device_id_type=MESH)

    each(1, NZ, lambda k: greet(to_z(k)))
    each(1, NY, lambda k: greet(to_y(k)))
    each(1, NX, lambda k: greet(to_x(k)))
    greet(twin)
    pl.semaphore_wait(barrier, NZ + NY + NX - 2)

    def own(k):
        return copy(ql, ag.at[y, z], agz_s.at[k], agz_r.at[k], to_z(k))

    def beside(k, up):
        block = ag.at[y, zat(-k)]
        if up:
            return copy(block, block, yp_s.at[k], yp_r.at[k], to_y(1))
        return copy(block, block, ym_s.at[k], ym_r.at[k], to_y(3))

    loads[0].wait()
    push_near(own)
    beside(0, True).start()
    beside(0, False).start()
    sends.append(lambda: each(0, NZ, lambda k: beside(k, True).wait_send()))
    sends.append(lambda: each(0, NZ, lambda k: beside(k, False).wait_send()))

    loads[1].wait()

    def permute(i, _):
        rows = pl.ds(pl.multiple_of(i * 256, 256), 256)
        w = wuq_v[rows, :]
        wp[rows, 0:128] = w[:, 0:128]
        wp[rows, 128:256] = w[:, 192:320]
        wp[rows, 256:384] = jnp.concatenate([w[:, 128:192], w[:, 320:384]], axis=1)
        return 0

    lax.fori_loop(0, QL // 256, permute, 0)

    def handed(i):
        k = near(i)
        landed(ag.at[y, zat(-k)], agz_s.at[k], agz_r.at[k])
        beside(k, True).start()
        beside(k, False).start()

    each(1, NZ, handed)

    push_near(
        lambda k: copy(
            wkup.at[pl.ds(krow, 32), :],
            wk.at[z, pl.ds(krow, 32), :],
            kz_s.at[k],
            kz_r.at[k],
            to_z(k),
        )
    )

    def queries(k):
        yy = yat(k)
        q = nn(ag[yy].reshape(NZ * RQ, QL), wp[...]).astype(BF16)
        qb[yy] = q.reshape(NZ, RQ, 384)
        zq[z, yy] = qb[yy, z]
        push_near(
            lambda j: copy(
                qb.at[yy, zat(j)], zq.at[z, yy], qz_s.at[k, j], qz_r.at[k, j], to_z(j)
            )
        )

    queries(0)

    def relay(k, up):
        block = ag.at[yat(-1 if up else 1), zat(-k)]
        return copy(block, block, f_s.at[k], f_r.at[k], to_y(1 if up else 3))

    def rows_beside(k, up):
        zs = zat(-k)
        landed(ag.at[yat(-1), zs], yp_s.at[k], yp_r.at[k])
        landed(ag.at[yat(1), zs], ym_s.at[k], ym_r.at[k])
        relay(k, up).start()

    def pair(k):
        rows_beside(k, False)
        rows_beside(NZ - k, True)

    rows_beside(0, True)
    each(1, NZ // 2, pair)
    rows_beside(NZ // 2, False)
    sends.append(lambda: each(0, NZ, lambda k: relay(k, True).wait_send()))

    queries(1)
    queries(3)

    loads[2].wait()
    each(
        1,
        NZ,
        lambda k: landed(wk.at[zat(-k), pl.ds(krow, 32), :], kz_s.at[k], kz_r.at[k]),
    )

    def wk_x(k):
        block = wk.at[:, pl.ds(krow, 32), :]
        return copy(block, block, kx_s.at[k], kx_r.at[k], to_x(k))

    push_x(wk_x)

    live = plen[0]

    def prefix(k, h):
        yy = yat(k)
        hc = slice(h * 128, (h + 1) * 128)
        q = qb[yy].reshape(NZ * RQ, 384)
        qn = q[:, hc]
        qr = q[:, 256 + h * ROPE : 256 + (h + 1) * ROPE]

        def score(t, m):
            t0 = pl.multiple_of(t * TB, TB)
            s = nt(qn, keys[pl.ds(t0, TB), hc]) + nn(qr, rope[:, pl.ds(t0, TB)])
            col = t0 + lax.broadcasted_iota(jnp.int32, s.shape, 1)
            s = jnp.where(col < live, s * SCALE2, -jnp.inf)
            sc[:, pl.ds(t0, TB)] = s
            for j in range(TB // 128):
                m = jnp.maximum(m, s[:, j * 128 : (j + 1) * 128])
            return m

        m = lax.fori_loop(0, PREFIX // TB, score, jnp.full((128, 128), -jnp.inf, F32))
        top = jnp.max(m, axis=1, keepdims=True)

        def weigh(t, carry):
            acc, den = carry
            t0 = pl.multiple_of(t * TB, TB)
            p = jnp.exp2(sc[:, pl.ds(t0, TB)] - top)
            for j in range(TB // 128):
                den = den + p[:, j * 128 : (j + 1) * 128]
            return acc + nn(p.astype(BF16), vals[pl.ds(t0, TB), hc]), den

        zero = jnp.zeros((128, 128), F32)
        acc, den = lax.fori_loop(0, PREFIX // TB, weigh, (zero, zero))
        den = jnp.sum(den, axis=1, keepdims=True)
        po[h, yy] = (acc / den).reshape(NZ, RQ, VD)
        lse2 = jnp.broadcast_to(top + jnp.log(den) * math.log2(math.e), (128, 128))
        plse[h, yy] = lse2.reshape(NZ, RQ, 128)

    loads[4].wait()
    loads[5].wait()
    loads[6].wait()
    prefix(0, 0)

    each(0, NZ, lambda k: landed(ag.at[yat(2), zat(-k)], f_s.at[k], f_r.at[k]))
    queries(2)

    push_near(
        lambda k: copy(
            wvup.at[pl.ds(vrow, 128), pl.ds(vcol, 128)],
            wv.at[z, c, pl.ds(vrow, 128), :],
            vz_s.at[k],
            vz_r.at[k],
            to_z(k),
        )
    )

    prefix(0, 1)

    def wk_landed(k):
        rows = pl.ds(pl.multiple_of(c * 128 + lax.rem(x - k + NX, NX) * 32, 32), 32)
        landed(wk.at[:, rows, :], kx_s.at[k], kx_r.at[k])

    each(1, NX, wk_landed)
    half = wk.at[:, pl.ds(vcol, 128), :]
    push(half, half, kc_s.at[0], kc_r.at[0], twin)

    def arrive(k):
        each(1, NZ, lambda j: landed(zq.at[zat(-j), yat(k)], qz_s.at[k, j], qz_r.at[k, j]))

    def absorb(ks):
        def one(zz, _):
            q = jnp.concatenate([zq[zz, yat(k)] for k in ks], axis=0)
            rows = pl.ds(pl.multiple_of(zz * RQ, RQ), RQ)
            for h in range(2):
                hc = slice(h * 128, (h + 1) * 128)
                a = nn(q[:, hc], wk[zz, hc, :]).astype(BF16)
                for i, k in enumerate(ks):
                    absb[yat(k), h, rows, :] = a[i * RQ : (i + 1) * RQ]
            for i, k in enumerate(ks):
                rps[yat(k), rows, :] = q[i * RQ : (i + 1) * RQ, 256:384]
            return 0

        lax.fori_loop(0, NZ, one, 0)
        for k in ks:
            if k:
                yy = yat(k)
                push(absb.at[yy], rec1.at[y], a_s.at[k], a_r.at[k], to_y(k))
                push(rps.at[yy], rec1r.at[y], ar_s.at[k], ar_r.at[k], to_y(k))

    arrive(1)
    arrive(3)
    landed(wk.at[:, pl.ds(ccol, 128), :], kc_s.at[0], kc_r.at[0])
    absorb((1, 3))
    arrive(0)
    arrive(2)
    absorb((2, 0))

    loads[3].wait()
    each(
        1,
        NZ,
        lambda k: landed(wv.at[zat(-k), c, pl.ds(vrow, 128), :], vz_s.at[k], vz_r.at[k]),
    )

    def wv_x(k):
        block = wv.at[:, c, pl.ds(vrow, 128), :]
        return copy(block, block, vx_s.at[k], vx_r.at[k], to_x(k))

    push_x(wv_x)


    def spread(k, src, srcr):
        yy = yat(k)
        for h in range(2):
            rows = pl.ds(pl.multiple_of(h * 512 + yy * 128, 128), 128)
            for j in range(4):
                qf[j, rows, :] = src[h, :, j * 128 : (j + 1) * 128].astype(F32)
        qrf[pl.ds(pl.multiple_of(yy * 128, 128), 128), :] = srcr[...].astype(F32)

    spread(0, absb.at[y], rps.at[y])
    prefix(1, 0)
    prefix(1, 1)
    prefix(3, 0)
    prefix(3, 1)


    def wv_landed(k):
        rows = pl.ds(pl.multiple_of(lax.rem(x - k + NX, NX) * 128, 128), 128)
        landed(wv.at[:, c, rows, :], vx_s.at[k], vx_r.at[k])

    each(1, NX, wv_landed)
    half = wv.at[:, c]
    push(half, half, vc_s.at[0], vc_r.at[0], twin)

    loads[7].wait()
    for k in range(1, NY):
        yy = yat(-k)
        landed(rec1.at[yy], a_s.at[k], a_r.at[k])
        landed(rec1r.at[yy], ar_s.at[k], ar_r.at[k])
        spread(-k, rec1.at[yy], rec1r.at[yy])

    lse[...] = jnp.zeros_like(lse)

    def private(r, _):
        q = jnp.concatenate([qf[j, pl.ds(r, 64, stride=RQ), :] for j in range(4)], axis=1)
        q = q.astype(BF16)
        qr = qrf[pl.ds(r, 32, stride=RQ), :]
        qr = jnp.concatenate([qr[:, :ROPE], qr[:, ROPE:]], axis=0).astype(BF16)
        s = nn(q, cache[r, :KVL, :]) + nn(qr, cache[r, KVL:, :])
        col = lax.broadcasted_iota(jnp.int32, s.shape, 1)
        s = jnp.where(col < lens[r], s * SCALE2, -jnp.inf)
        top = jnp.max(s, axis=1, keepdims=True)
        p = jnp.exp2(s - top)
        den = jnp.sum(p, axis=1, keepdims=True)
        latent = nt(p.astype(BF16), cache[r, :KVL, :]) / den
        for j in range(4):
            lf[j, pl.ds(r, 64, stride=RQ), :] = latent[:, j * 128 : (j + 1) * 128]
        lse2 = (top + jnp.log(den) * math.log2(math.e)).reshape(2, NY, NZ, 1)
        lane = lax.broadcasted_iota(jnp.int32, lse.shape, 3)
        lse[...] = jnp.where(lane == r, lse2, lse[...])
        return 0

    lax.fori_loop(0, RQ, private, 0, unroll=2)

    def gather(k, dst):
        yy = yat(k)
        for h in range(2):
            rows = pl.ds(pl.multiple_of(h * 512 + yy * 128, 128), 128)
            for j in range(4):
                dst[h, :, j * 128 : (j + 1) * 128] = lf[j, rows, :].astype(BF16)

    for k in (2, 1, 3):
        yy = yat(k)
        gather(k, send2.at[yy])
        push(send2.at[yy], rec2.at[y], b_s.at[k], b_r.at[k], to_y(k))
        push(lse.at[:, yy], recl.at[y], bl_s.at[k], bl_r.at[k], to_y(k))
    gather(0, rec2.at[y])
    recl[y] = lse[:, y]

    prefix(2, 0)
    prefix(2, 1)

    landed(wv.at[:, 1 - c], vc_s.at[0], vc_r.at[0])
    for k in range(1, NY):
        landed(recl.at[yat(-k)], bl_s.at[k], bl_r.at[k])
        landed(rec2.at[yat(-k)], b_s.at[k], b_r.at[k])
    total = recl[0]
    total = total.reshape(16, 128)
    for yy in range(1, NY):
        total = total + pltpu.roll(recl[yy].reshape(16, 128), yy * RQ, 1)
    mbuf[...] = total
    recm[z] = total
    push_near(lambda k: copy(mbuf, recm.at[z], cm_s.at[k], cm_r.at[k], to_z(k)))

    def project(zz, dst):
        rows = pl.ds(pl.multiple_of(zz * RQ, RQ), RQ)
        for h in range(2):
            lat = jnp.concatenate([rec2[yy, h, rows, :] for yy in range(NY)], axis=0)
            dst[zz, h] = nn(lat, wv[zz, h]).astype(BF16)

    def heads(k):
        return copy(outz.at[zat(k)], recz.at[z], c_s.at[k], c_r.at[k], to_z(k))

    def give(i):
        k = near(NZ - i)
        project(zat(k), outz)
        heads(k).start()

    each(1, NZ, give)
    sends.append(lambda: each(1, NZ, lambda k: heads(k).wait_send()))
    project(z, recz)

    def merge(zz):
        diag = lax.broadcasted_iota(jnp.int32, (64, 128), 0) == lax.broadcasted_iota(
            jnp.int32, (64, 128), 1
        )
        for h in range(2):
            row = jnp.broadcast_to(recm[zz, pl.ds(h * NZ + z, 1), :], (64, 128))
            plane = jnp.sum(jnp.where(diag, row, 0.0), axis=1, keepdims=True)
            mine = jnp.concatenate([po[h, yy, zz] for yy in range(NY)], axis=0)
            mine_lse = jnp.concatenate([plse[h, yy, zz] for yy in range(NY)], axis=0)
            upper = jnp.maximum(mine_lse, plane)
            first = jnp.exp2(mine_lse - upper)
            second = jnp.exp2(plane - upper)
            theirs = recz[zz, h].astype(F32)
            merged = ((first * mine + second * theirs) / (first + second)).astype(BF16)
            for yy in range(NY):
                rows = pl.ds(pl.multiple_of(yy * 128 + zz * RQ, RQ), RQ)
                out[rows, h * 128 : (h + 1) * 128] = merged[yy * RQ : (yy + 1) * RQ]

    def finish(i):
        k = near(i)
        zz = zat(-k)
        landed(recm.at[zz], cm_s.at[k], cm_r.at[k])
        landed(recz.at[zz], c_s.at[k], c_r.at[k])
        merge(zz)

    merge(z)
    each(1, NZ, finish)
    for wait in sends:
        wait()


def body(
    q_latent,
    w_uq,
    w_kup,
    w_vup,
    prefix_keys,
    prefix_values,
    prefix_rope,
    private_cache,
    lengths,
    prefix_len,
):
    cache = jnp.transpose(private_cache, (0, 2, 1))
    vm = pltpu.VMEM
    dma = pltpu.SemaphoreType.DMA
    hbm = pl.BlockSpec(memory_space=pl.ANY)
    smem = pl.BlockSpec(memory_space=pltpu.SMEM)
    scratch = [
        vm((QL, 384), BF16),
        vm((QL, 384), BF16),
        vm((PREFIX, 256), BF16),
        vm((PREFIX, 256), BF16),
        vm((ROPE, PREFIX), BF16),
        vm((RQ, KVL + ROPE, SLOTS), BF16),
        vm((NY, NZ, RQ, QL), BF16),
        vm((NY, NZ, RQ, 384), BF16),
        vm((NZ, NY, RQ, 384), BF16),
        vm((NZ, 256, KVL), BF16),
        vm((NZ, 2, KVL, VD), BF16),
        vm((NY, 2, NZ * RQ, KVL), BF16),
        vm((NY, NZ * RQ, 128), BF16),
        vm((NY, 2, NZ * RQ, KVL), BF16),
        vm((NY, NZ * RQ, 128), BF16),
        vm((4, 1024, 128), F32),
        vm((512, 128), F32),
        vm((4, 1024, 128), F32),
        vm((2, NY, NZ, 128), F32),
        vm((NY, 2, NZ * RQ, KVL), BF16),
        vm((NY, 2, NZ * RQ, KVL), BF16),
        vm((NY, 2, NZ, 128), F32),
        vm((NZ, 2, 64, VD), BF16),
        vm((16, 128), F32),
        vm((NZ, 2, 64, VD), BF16),
        vm((NZ, 16, 128), F32),
        vm((128, PREFIX), F32),
        vm((2, NY, NZ, RQ, VD), F32),
        vm((2, NY, NZ, RQ, 128), F32),
        dma((8,)),
    ]
    sems = [8, 8, 8, 8, 8, 8, 8, 8, (4, 8), (4, 8), 8, 8, 4, 4, 1, 1, 8, 8, 4, 4, 1, 1]
    sems += [4] * 8 + [8] * 4
    scratch += [dma(n if isinstance(n, tuple) else (n,)) for n in sems]
    return pl.pallas_call(
        kernel,
        out_shape=jax.ShapeDtypeStruct((512, 256), BF16),
        in_specs=[hbm] * 8 + [smem] * 2,
        out_specs=pl.BlockSpec(memory_space=vm),
        scratch_shapes=scratch,
        compiler_params=pltpu.CompilerParams(
            collective_id=0, has_side_effects=True, vmem_limit_bytes=58 * 2**20
        ),
        cost_estimate=pl.CostEstimate(
            flops=5 * 10**9, bytes_accessed=14 * 10**6, transcendentals=5 * 10**6
        ),
        name="latent_attention",
    )(
        q_latent, w_uq, w_kup, w_vup, prefix_keys, prefix_values, prefix_rope, cache, lengths,
        prefix_len,
    )


def solution(mesh):
    placed = (
        P(("grp", "dev"), None),
        P(None, "dev"),
        P("dev", None),
        P(None, "dev"),
        P("grp", "dev"),
        P("grp", "dev"),
        P(None, "grp"),
        P(("grp", "dev"), None, None),
        P(("grp", "dev")),
        P("grp"),
    )
    return jax.shard_map(
        body, mesh=mesh, in_specs=placed, out_specs=P("grp", "dev"), check_vma=False
    )
```

time: 199 us -> 98.9 us (0.50)
  Pallas kernels: 0 us -> 94.8 us
  waiting for transfers between devices: 93.7 us -> 0 us
  matrix products: 42.7 us -> 0 us
  starting transfers between devices: 19 us -> 0 us
  local copies, waits for them, and re-layouts: 19.4 us -> 1.67 us
  between operations: 14.2 us -> 0.66 us
  other arithmetic: 9.01 us -> 0 us
    pallas_call x0 -> x1, Pallas kernels: none -> 94.8 us  [body(): pl.pallas_call(kernel, out_shape=jax.ShapeDtypeStruct((512, 256), BF16),...]
    all_gather x1 -> x0, waiting for transfers between devices: 82.2 us -> none  [body(): lax.all_gather(q_latent, 'dev', axis=0, tiled=True)]
    dot_general x8 -> x0, matrix products: 42.7 us -> none  [the longest x1 10.9 us: body(): jnp.einsum('rhn,thn->hrt', q_nope, key_heads, preferred_element_type=jnp....]
    all_to_all x3 -> x0, starting transfers between devices: 19 us -> none  [the longest x1 6.54 us: body(): lax.all_to_all(lse_here.astype(jnp.bfloat16), 'dev', split_axis=0, concat...]
    all_to_all x3 -> x0, waiting for transfers between devices: 10.8 us -> none  [the longest x1 4.22 us: body(): lax.all_to_all(latent, 'dev', split_axis=0, concat_axis=1, tiled=True)]
    reduce_sum x2 -> x0, other arithmetic: 8.81 us -> none  [the longest x1 8.25 us: body(): prefix_den = jnp.sum(prefix_exp, axis=2)]
    reshape x2 -> x0, local copies, waits for them, and re-layouts: 5.88 us -> none  [the longest x1 4.08 us: body(): value_heads = prefix_values.reshape(prefix_slots, head_dev, VD)]
    all_to_all x4 -> x0, local copies, waits for them, and re-layouts: 5.84 us -> none  [the longest x3 5.77 us: body(): lax.all_to_all(sent, 'dev', split_axis=1, concat_axis=0, tiled=True)]
  transfers between devices with their start and end apart: 4 -> 0, of which waited for: 4 -> 0; matrix products, arithmetic and copies ran while one was open for 26% -> 0% of each run, Pallas kernels for 0% -> 0%
where the time goes in v1:
time: 98.9 us; the launch traced here: 97.2 us
  Pallas kernels  94.8 us (96%)
  local copies, waits for them, and re-layouts  1.67 us (2%)
    pallas_call x1, Pallas kernels, body(): pl.pallas_call(kernel, out_shape=jax.ShapeDtypeStruct((512, 256), BF16),...  94.8 us

profile of v1, /device:TPU:6, one launch (start us, length us, event | category | flops | bytes accessed | tf_op | source)
XLA Modules:
  0.0 97.2 jit_solution(15089362195383424777)
XLA Ops:
  0.7 94.8 %latent_attention.1 = bf16[512,256]{1,0:T(8,128)(2,1)} custom-call(bf16[16,1536]{1,0:T(8,128)(2,1)} %ql.1, bf16[1536,384]{1,0:T(8,128)(2,1)} %wuq.1, bf16[256,512]{1,0:T(8,128)(2,1)} %wkup.1, bf16[512,256]{1,0:T(8,128)(2,1)} %wvup.1, bf16[4096,256]{1,0:T(8,128)(2,1)} %keys_h.1, bf16[4096,256]{1,0:T(8,128)(2,1)} %vals_h.1, bf16[64,4096]{1,0:T(8,128)(2,1)} %rope_h.1, ...), custom_call_target="tpu_custom_call" | custom-call | flops 5000000000 | bytes 14000000 | tf_op jit(solution)/shard_map/latent_attention/pallas_call | solution.py:522
  95.5 1.7 %copy.13 = bf16[512,256]{1,0:T(8,128)(2,1)} copy(bf16[512,256]{1,0:T(8,128)(2,1)} %latent_attention.1) | data formatting | bytes 524288

commit v2 on v1

v2 whole, which is shorter than its diff:
```python
import math

import jax
import jax.numpy as jnp
from jax import lax
from jax.experimental import pallas as pl
from jax.experimental.pallas import tpu as pltpu
from jax.sharding import PartitionSpec as P

KVL = 512
NOPE = 128
ROPE = 64
VD = 128
MESH = pl.DeviceIdType.MESH
NY, NZ, NX = 4, 8, 4
RQ = 16
RH = 8
SLOTS = 384
PREFIX = 4096
QL = 1536
TB = 512
SCALE2 = math.log2(math.e) / math.sqrt(NOPE + ROPE)
F32 = jnp.float32
BF16 = jnp.bfloat16


def nn(a, b):
    return lax.dot_general(a, b, (((1,), (0,)), ((), ())), preferred_element_type=F32)


def nt(a, b):
    return lax.dot_general(a, b, (((1,), (1,)), ((), ())), preferred_element_type=F32)


def near(i):
    odd = lax.rem(i, 2)
    return odd * lax.div(i + 1, 2) + (1 - odd) * (NZ - lax.div(i, 2))


def each(low, high, step):
    def one(i, carry):
        step(i)
        return carry

    lax.fori_loop(low, high, one, 0)


def kernel(
    ql, wuq, wkup, wvup, keys_h, vals_h, rope_h, cache_h, lens, plen, out,
    wuq_v, wp, keys, vals, rope, cache, ag, qb, zq, wk, wv, absb, rps, rec1, rec1r,
    qf, qrf, lf, lse, send2, rec2, recl, outz, mbuf, recz, recm, half0, sc, po, plse,
    ld, agz_s, agz_r, yp_s, yp_r, ym_s, ym_r, f_s, f_r, qz_s, qz_r,
    kz_s, kz_r, kc_s, kc_r, vz_s, vz_r, vx_s, vx_r, vc_s, vc_r,
    a_s, a_r, ar_s, ar_r, b_s, b_r, bl_s, bl_r, c_s, c_r, cm_s, cm_r,
):
    g = lax.axis_index("grp")
    d = lax.axis_index("dev")
    x, c = lax.div(g, 2), lax.rem(g, 2)
    y, z = lax.div(d, NZ), lax.rem(d, NZ)

    def yat(k):
        return lax.rem(y + (k + NY), NY)

    def zat(k):
        return lax.rem(z + (k + NZ), NZ)

    def to_y(k):
        return (g, yat(k) * NZ + z)

    def to_z(k):
        return (g, y * NZ + zat(k))

    def to_x(k):
        return (lax.rem(x + k, NX) * 2 + c, d)

    twin = (x * 2 + 1 - c, d)
    sends = []

    def copy(src, dst, ss, rs, dev):
        return pltpu.make_async_remote_copy(
            src_ref=src, dst_ref=dst, send_sem=ss, recv_sem=rs, device_id=dev, device_id_type=MESH
        )

    def push(*what):
        one = copy(*what)
        one.start()
        sends.append(one.wait_send)

    def push_near(what):
        each(1, NZ, lambda i: what(near(i)).start())
        sends.append(lambda: each(1, NZ, lambda i: what(i).wait_send()))

    def push_x(what):
        each(1, NX, lambda i: what(i).start())
        sends.append(lambda: each(1, NX, lambda i: what(i).wait_send()))

    def landed(dst, ss, rs):
        pltpu.make_async_remote_copy(
            src_ref=dst, dst_ref=dst, send_sem=ss, recv_sem=rs, device_id=twin, device_id_type=MESH
        ).wait_recv()

    vrow = pl.multiple_of(x * 128, 128)
    vcol = pl.multiple_of(c * 128, 128)
    ccol = pl.multiple_of((1 - c) * 128, 128)

    loads = [
        pltpu.make_async_copy(ql, ag.at[y, z], ld.at[0]),
        pltpu.make_async_copy(wuq, wuq_v, ld.at[1]),
        pltpu.make_async_copy(wkup.at[pl.ds(vcol, 128), :], wk.at[z, pl.ds(vcol, 128), :], ld.at[2]),
        pltpu.make_async_copy(
            wvup.at[pl.ds(vrow, 128), pl.ds(vcol, 128)],
            wv.at[z, c, pl.ds(vrow, 128), :],
            ld.at[3],
        ),
        pltpu.make_async_copy(keys_h, keys, ld.at[4]),
        pltpu.make_async_copy(rope_h, rope, ld.at[5]),
        pltpu.make_async_copy(vals_h, vals, ld.at[6]),
        pltpu.make_async_copy(cache_h, cache, ld.at[7]),
    ]
    for load in loads:
        load.start()

    barrier = pltpu.get_barrier_semaphore()

    def greet(dev):
        pl.semaphore_signal(barrier, inc=1, device_id=dev, device_id_type=MESH)

    each(1, NZ, lambda k: greet(to_z(k)))
    each(1, NY, lambda k: greet(to_y(k)))
    each(1, NX, lambda k: greet(to_x(k)))
    greet(twin)

    loads[1].wait()

    def permute(i, _):
        rows = pl.ds(pl.multiple_of(i * 256, 256), 256)
        w = wuq_v[rows, :]
        wp[rows, 0:128] = w[:, 0:128]
        wp[rows, 128:256] = w[:, 192:320]
        wp[rows, 256:384] = jnp.concatenate([w[:, 128:192], w[:, 320:384]], axis=1)
        return 0

    lax.fori_loop(0, QL // 256, permute, 0)
    loads[0].wait()
    loads[2].wait()
    loads[3].wait()
    pl.semaphore_wait(barrier, NZ + NY + NX - 2)

    def place(h, up):
        return (zat(-h), h) if up else (zat(h), NZ - h)

    def ring(h, up, view, ss, rs):
        zs, _ = place(h - 1, up)
        k = h if up else NZ - h
        return copy(view(zs), view(zs), ss.at[k], rs.at[k], to_z(1 if up else NZ - 1))

    def ag_view(zs):
        return ag.at[y, zs]

    def wk_view(zs):
        return wk.at[zs, pl.ds(vcol, 128), :]

    def wv_view(zs):
        return wv.at[zs, c, pl.ds(vrow, 128), :]

    tables = ((ag_view, agz_s, agz_r, 4, 3), (wk_view, kz_s, kz_r, 3, 4), (wv_view, vz_s, vz_r, 4, 3))

    def beside(k, up):
        block = ag.at[y, zat(-k)]
        if up:
            return copy(block, block, yp_s.at[k], yp_r.at[k], to_y(1))
        return copy(block, block, ym_s.at[k], ym_r.at[k], to_y(3))

    def hop(h, table):
        view, ss, rs, far_up, far_down = table
        for up, far in ((True, far_up), (False, far_down)):
            if h > 1 and h - 1 <= far:
                zs, k = place(h - 1, up)
                landed(view(zs), ss.at[k], rs.at[k])
            if h <= far:
                one = ring(h, up, view, ss, rs)
                one.start()
                sends.append(one.wait_send)
            if view is ag_view and h - 1 <= far and (h > 1 or up):
                _, k = place(h - 1, up)
                k %= NZ
                beside(k, True).start()
                beside(k, False).start()

    sends.append(lambda: each(0, NZ, lambda k: beside(k, True).wait_send()))
    sends.append(lambda: each(0, NZ, lambda k: beside(k, False).wait_send()))

    def relay(k, up):
        block = ag.at[yat(-1 if up else 1), zat(-k)]
        return copy(block, block, f_s.at[k], f_r.at[k], to_y(1 if up else 3))

    def rows_beside(k, up):
        zs = zat(-k)
        landed(ag.at[yat(-1), zs], yp_s.at[k], yp_r.at[k])
        landed(ag.at[yat(1), zs], ym_s.at[k], ym_r.at[k])
        relay(k, up).start()

    def pair(k):
        rows_beside(k, False)
        rows_beside(NZ - k, True)

    sends.append(lambda: each(0, NZ, lambda k: relay(k, True).wait_send()))

    for h in range(1, 6):
        for table in tables:
            hop(h, table)
        if h == 2:
            rows_beside(0, True)
        elif h > 2:
            pair(h - 2)

    half = wk.at[:, pl.ds(vcol, 128), :]
    push(half, half, kc_s.at[0], kc_r.at[0], twin)

    def wv_x(k):
        block = wv.at[:, c, pl.ds(vrow, 128), :]
        return copy(block, block, vx_s.at[k], vx_r.at[k], to_x(k))

    push_x(wv_x)

    def queries(k):
        yy = yat(k)
        q = nn(ag[yy].reshape(NZ * RQ, QL), wp[...]).astype(BF16)
        qb[yy] = q.reshape(NZ, RQ, 384)
        zq[z, yy] = qb[yy, z]
        push_near(
            lambda j: copy(
                qb.at[yy, zat(j)], zq.at[z, yy], qz_s.at[k, j], qz_r.at[k, j], to_z(j)
            )
        )

    queries(0)
    rows_beside(NZ // 2, False)
    queries(1)
    queries(3)

    live = plen[0]

    def prefix(k, h):
        yy = yat(k)
        hc = slice(h * 128, (h + 1) * 128)
        q = qb[yy].reshape(NZ * RQ, 384)
        qn = q[:, hc]
        qr = q[:, 256 + h * ROPE : 256 + (h + 1) * ROPE]

        def score(t, m):
            t0 = pl.multiple_of(t * TB, TB)
            s = nt(qn, keys[pl.ds(t0, TB), hc]) + nn(qr, rope[:, pl.ds(t0, TB)])
            col = t0 + lax.broadcasted_iota(jnp.int32, s.shape, 1)
            s = jnp.where(col < live, s * SCALE2, -jnp.inf)
            sc[:, pl.ds(t0, TB)] = s
            for j in range(TB // 128):
                m = jnp.maximum(m, s[:, j * 128 : (j + 1) * 128])
            return m

        m = lax.fori_loop(0, PREFIX // TB, score, jnp.full((128, 128), -jnp.inf, F32))
        top = jnp.max(m, axis=1, keepdims=True)

        def weigh(t, carry):
            acc, den = carry
            t0 = pl.multiple_of(t * TB, TB)
            p = jnp.exp2(sc[:, pl.ds(t0, TB)] - top)
            for j in range(TB // 128):
                den = den + p[:, j * 128 : (j + 1) * 128]
            return acc + nn(p.astype(BF16), vals[pl.ds(t0, TB), hc]), den

        zero = jnp.zeros((128, 128), F32)
        acc, den = lax.fori_loop(0, PREFIX // TB, weigh, (zero, zero))
        den = jnp.sum(den, axis=1, keepdims=True)
        po[h, yy] = (acc / den).reshape(NZ, RQ, VD)
        lse2 = jnp.broadcast_to(top + jnp.log(den) * math.log2(math.e), (128, 128))
        plse[h, yy] = lse2.reshape(NZ, RQ, 128)

    loads[4].wait()
    loads[5].wait()
    loads[6].wait()
    prefix(0, 0)

    each(0, NZ, lambda k: landed(ag.at[yat(2), zat(-k)], f_s.at[k], f_r.at[k]))
    queries(2)

    prefix(0, 1)

    def arrive(k):
        each(1, NZ, lambda j: landed(zq.at[zat(-j), yat(k)], qz_s.at[k, j], qz_r.at[k, j]))

    def absorb(ks):
        def one(zz, _):
            q = jnp.concatenate([zq[zz, yat(k)] for k in ks], axis=0)
            rows = pl.ds(pl.multiple_of(zz * RQ, RQ), RQ)
            a = [nn(q[:, h * 128 : (h + 1) * 128], wk[zz, h * 128 : (h + 1) * 128, :]) for h in range(2)]
            for i, k in enumerate(ks):
                for t in range(2):
                    part = slice(i * RQ + t * RH, i * RQ + (t + 1) * RH)
                    both = jnp.concatenate([a[0][part], a[1][part]], axis=0)
                    absb[t, yat(k), rows, :] = both.astype(BF16)
                rps[yat(k), rows, :] = q[i * RQ : (i + 1) * RQ, 256:384]
            return 0

        lax.fori_loop(0, NZ, one, 0)

    def send_absorbed(t, k):
        push(absb.at[t, yat(k)], rec1.at[t, y], a_s.at[t, k], a_r.at[t, k], to_y(k))

    def send_rotary(k):
        push(rps.at[yat(k)], rec1r.at[y], ar_s.at[k], ar_r.at[k], to_y(k))

    arrive(1)
    arrive(3)
    landed(wk.at[:, pl.ds(ccol, 128), :], kc_s.at[0], kc_r.at[0])
    absorb((1, 3))
    for k in (1, 3):
        send_rotary(k)
        send_absorbed(0, k)
    arrive(0)
    arrive(2)
    absorb((2, 0))
    send_rotary(2)
    send_absorbed(0, 2)
    for k in (1, 3, 2):
        send_absorbed(1, k)

    def spread(t, k, src):
        rows = pl.ds(pl.multiple_of(yat(k) * 128, 128), 128)
        for j in range(4):
            qf[t, j, rows, :] = src[:, j * 128 : (j + 1) * 128].astype(F32)

    def spread_rotary(k, src):
        base = yat(k) * 128
        for zz in range(NZ):
            tile = src[zz * RQ : (zz + 1) * RQ, :].astype(F32)
            for h in range(2):
                part = tile[:, h * ROPE : (h + 1) * ROPE]
                rows = pl.ds(pl.multiple_of(base + (zz * 2 + h) * RH, RH), RH)
                for t in range(2):
                    qrf[t, rows, 0:ROPE] = part[t * RH : (t + 1) * RH]

    spread_rotary(0, rps.at[y])
    spread(0, 0, absb.at[0, y])
    spread(1, 0, absb.at[1, y])
    prefix(1, 0)
    prefix(1, 1)

    def wv_landed(k):
        rows = pl.ds(pl.multiple_of(lax.rem(x - k + NX, NX) * 128, 128), 128)
        landed(wv.at[:, c, rows, :], vx_s.at[k], vx_r.at[k])

    each(1, NX, wv_landed)
    half = wv.at[:, c]
    push(half, half, vc_s.at[0], vc_r.at[0], twin)

    lse[...] = jnp.zeros_like(lse)
    loads[7].wait()
    for k in range(1, NY):
        yy = yat(-k)
        landed(rec1r.at[yy], ar_s.at[k], ar_r.at[k])
        spread_rotary(-k, rec1r.at[yy])

    def attend(t):
        for k in range(1, NY):
            yy = yat(-k)
            landed(rec1.at[t, yy], a_s.at[t, k], a_r.at[t, k])
            spread(t, -k, rec1.at[t, yy])

        def private(i, _):
            r = t * RH + i
            mine = pl.ds(i, 64, stride=RH)
            q = jnp.concatenate([qf[t, j, mine, :] for j in range(4)], axis=1).astype(BF16)
            qr = qrf[t, mine, :][:, :ROPE].astype(BF16)
            s = nn(q, cache[r, :KVL, :]) + nn(qr, cache[r, KVL:, :])
            col = lax.broadcasted_iota(jnp.int32, s.shape, 1)
            s = jnp.where(col < lens[r], s * SCALE2, -jnp.inf)
            top = jnp.max(s, axis=1, keepdims=True)
            p = jnp.exp2(s - top)
            den = jnp.sum(p, axis=1, keepdims=True)
            latent = nt(p.astype(BF16), cache[r, :KVL, :]) / den
            for j in range(4):
                lf[j, mine, :] = latent[:, j * 128 : (j + 1) * 128]
            lse2 = (top + jnp.log(den) * math.log2(math.e)).reshape(NY, 16, 1)
            lane = lax.broadcasted_iota(jnp.int32, lse.shape[1:], 2)
            lse[t] = jnp.where(lane == r, lse2, lse[t])
            return 0

        lax.fori_loop(0, RH, private, 0, unroll=2)

        def gather(k, dst):
            rows = pl.ds(pl.multiple_of(yat(k) * 128, 128), 128)
            for j in range(4):
                dst[:, j * 128 : (j + 1) * 128] = lf[j, rows, :].astype(BF16)

        for k in (2, 1, 3):
            yy = yat(k)
            gather(k, send2.at[t, yy])
            push(lse.at[t, yy], recl.at[t, y], bl_s.at[t, k], bl_r.at[t, k], to_y(k))
            push(send2.at[t, yy], rec2.at[t, y], b_s.at[t, k], b_r.at[t, k], to_y(k))
        gather(0, rec2.at[t, y])
        recl[t, y] = lse[t, y]

    attend(0)
    attend(1)
    prefix(3, 0)
    landed(wv.at[:, 1 - c], vc_s.at[0], vc_r.at[0])
    mbuf[...] = jnp.zeros_like(mbuf)

    def deliver(t):
        for k in range(1, NY):
            landed(recl.at[t, yat(-k)], bl_s.at[t, k], bl_r.at[t, k])
        total = recl[t, 0]
        for yy in range(1, NY):
            total = total + pltpu.roll(recl[t, yy], yy * RQ, 1)
        for zz in range(NZ):
            mbuf[t, zz, 0:2] = total[2 * zz : 2 * zz + 2]
        recm[t, z] = mbuf[t, z]
        push_near(lambda k: copy(mbuf.at[t, zat(k)], recm.at[t, z], cm_s.at[t, k], cm_r.at[t, k], to_z(k)))
        for k in range(1, NY):
            landed(rec2.at[t, yat(-k)], b_s.at[t, k], b_r.at[t, k])

        def project(zz, dst):
            rows = pl.ds(pl.multiple_of(zz * RQ, RQ), RQ)
            lat = jnp.concatenate([rec2[t, yy, rows, :] for yy in range(NY)], axis=0)
            for h in range(2):
                o = nn(lat, wv[zz, h]).reshape(NY, 2, RH, VD)[:, h].reshape(NY * RH, VD)
                dst[t, zz, h] = o.astype(BF16)

        def heads(k):
            return copy(outz.at[t, zat(k)], recz.at[t, z], c_s.at[t, k], c_r.at[t, k], to_z(k))

        def give(i):
            k = near(NZ - i)
            project(zat(k), outz)
            heads(k).start()

        each(1, NZ, give)
        sends.append(lambda: each(1, NZ, lambda k: heads(k).wait_send()))
        project(z, recz)

    deliver(0)
    prefix(3, 1)
    deliver(1)
    prefix(2, 0)
    prefix(2, 1)

    def merge(t, zz, h):
        diag = (
            lax.broadcasted_iota(jnp.int32, (NY, RH, 128), 0) * RQ
            + lax.broadcasted_iota(jnp.int32, (NY, RH, 128), 1)
            + t * RH
        ) == lax.broadcasted_iota(jnp.int32, (NY, RH, 128), 2)
        row = recm[t, zz, h : h + 1, :].reshape(1, 1, 128)
        plane = jnp.sum(jnp.where(diag, row, 0.0), axis=2, keepdims=True)
        part = slice(t * RH, (t + 1) * RH)
        mine = po[h, :, zz, part, :]
        mine_lse = plse[h, :, zz, part, :]
        upper = jnp.maximum(mine_lse, plane)
        first = jnp.exp2(mine_lse - upper)
        second = jnp.exp2(plane - upper)
        theirs = recz[t, zz, h].astype(F32).reshape(NY, RH, VD)
        return (first * mine + second * theirs) / (first + second)

    def early(zz):
        for h in range(2):
            half0[zz, h] = merge(0, zz, h)

    def late(zz):
        for h in range(2):
            both = jnp.concatenate([half0[zz, h], merge(1, zz, h)], axis=1).astype(BF16)
            for yy in range(NY):
                rows = pl.ds(pl.multiple_of(yy * 128 + zz * RQ, RQ), RQ)
                out[rows, h * 128 : (h + 1) * 128] = both[yy]

    def finish(t, step):
        def one(i):
            k = near(i)
            zz = zat(-k)
            landed(recm.at[t, zz], cm_s.at[t, k], cm_r.at[t, k])
            landed(recz.at[t, zz], c_s.at[t, k], c_r.at[t, k])
            step(zz)

        step(z)
        each(1, NZ, one)

    finish(0, early)
    finish(1, late)
    for wait in sends:
        wait()


def body(
    q_latent,
    w_uq,
    w_kup,
    w_vup,
    prefix_keys,
    prefix_values,
    prefix_rope,
    private_cache,
    lengths,
    prefix_len,
):
    cache = jnp.transpose(private_cache, (0, 2, 1))
    vm = pltpu.VMEM
    dma = pltpu.SemaphoreType.DMA
    hbm = pl.BlockSpec(memory_space=pl.ANY)
    smem = pl.BlockSpec(memory_space=pltpu.SMEM)
    scratch = [
        vm((QL, 384), BF16),
        vm((QL, 384), BF16),
        vm((PREFIX, 256), BF16),
        vm((PREFIX, 256), BF16),
        vm((ROPE, PREFIX), BF16),
        vm((RQ, KVL + ROPE, SLOTS), BF16),
        vm((NY, NZ, RQ, QL), BF16),
        vm((NY, NZ, RQ, 384), BF16),
        vm((NZ, NY, RQ, 384), BF16),
        vm((NZ, 256, KVL), BF16),
        vm((NZ, 2, KVL, VD), BF16),
        vm((2, NY, 128, KVL), BF16),
        vm((NY, NZ * RQ, 128), BF16),
        vm((2, NY, 128, KVL), BF16),
        vm((NY, NZ * RQ, 128), BF16),
        vm((2, 4, 512, 128), F32),
        vm((2, 512, 128), F32),
        vm((4, 512, 128), F32),
        vm((2, NY, 16, 128), F32),
        vm((2, NY, 128, KVL), BF16),
        vm((2, NY, 128, KVL), BF16),
        vm((2, NY, 16, 128), F32),
        vm((2, NZ, 2, NY * RH, VD), BF16),
        vm((2, NZ, 8, 128), F32),
        vm((2, NZ, 2, NY * RH, VD), BF16),
        vm((2, NZ, 8, 128), F32),
        vm((NZ, 2, NY, RH, VD), F32),
        vm((128, PREFIX), F32),
        vm((2, NY, NZ, RQ, VD), F32),
        vm((2, NY, NZ, RQ, 128), F32),
        dma((8,)),
    ]
    sems = [8, 8, 8, 8, 8, 8, 8, 8, (4, 8), (4, 8), 8, 8, 1, 1, 8, 8, 4, 4, 1, 1]
    sems += [(2, 4), (2, 4), 4, 4] + [(2, 4)] * 4 + [(2, 8)] * 4
    scratch += [dma(n if isinstance(n, tuple) else (n,)) for n in sems]
    return pl.pallas_call(
        kernel,
        out_shape=jax.ShapeDtypeStruct((512, 256), BF16),
        in_specs=[hbm] * 8 + [smem] * 2,
        out_specs=pl.BlockSpec(memory_space=vm),
        scratch_shapes=scratch,
        compiler_params=pltpu.CompilerParams(
            collective_id=0, has_side_effects=True, vmem_limit_bytes=58 * 2**20
        ),
        cost_estimate=pl.CostEstimate(
            flops=5 * 10**9, bytes_accessed=14 * 10**6, transcendentals=5 * 10**6
        ),
        name="latent_attention",
    )(
        q_latent, w_uq, w_kup, w_vup, prefix_keys, prefix_values, prefix_rope, cache, lengths,
        prefix_len,
    )


def solution(mesh):
    placed = (
        P(("grp", "dev"), None),
        P(None, "dev"),
        P("dev", None),
        P(None, "dev"),
        P("grp", "dev"),
        P("grp", "dev"),
        P(None, "grp"),
        P(("grp", "dev"), None, None),
        P(("grp", "dev")),
        P("grp"),
    )
    return jax.shard_map(
        body, mesh=mesh, in_specs=placed, out_specs=P("grp", "dev"), check_vma=False
    )
```

time: 98.9 us -> 84.2 us (0.85); the launches traced: 97.2 us -> 84.1 us
  Pallas kernels: 94.8 us -> 81.7 us
    pallas_call x1, Pallas kernels: 94.8 us -> 81.7 us  [body(): pl.pallas_call(kernel, out_shape=jax.ShapeDtypeStruct((512, 256), BF16),...]
where the time goes in v2:
time: 84.2 us; the launch traced here: 84.1 us
  Pallas kernels  81.7 us (97%)
  local copies, waits for them, and re-layouts  1.67 us (2%)
    pallas_call x1, Pallas kernels, body(): pl.pallas_call(kernel, out_shape=jax.ShapeDtypeStruct((512, 256), BF16),...  81.7 us

profile of v2, /device:TPU:6, one launch (start us, length us, event | category | flops | bytes accessed | tf_op | source)
XLA Modules:
  0.0 84.1 jit_solution(17797794298245368918)
XLA Ops:
  0.7 81.7 %latent_attention.1 = bf16[512,256]{1,0:T(8,128)(2,1)} custom-call(bf16[16,1536]{1,0:T(8,128)(2,1)} %ql.1, bf16[1536,384]{1,0:T(8,128)(2,1)} %wuq.1, bf16[256,512]{1,0:T(8,128)(2,1)} %wkup.1, bf16[512,256]{1,0:T(8,128)(2,1)} %wvup.1, bf16[4096,256]{1,0:T(8,128)(2,1)} %keys_h.1, bf16[4096,256]{1,0:T(8,128)(2,1)} %vals_h.1, bf16[64,4096]{1,0:T(8,128)(2,1)} %rope_h.1, ...), custom_call_target="tpu_custom_call" | custom-call | flops 5000000000 | bytes 14000000 | tf_op jit(solution)/shard_map/latent_attention/pallas_call | solution.py:546
  82.4 1.7 %copy.13 = bf16[512,256]{1,0:T(8,128)(2,1)} copy(bf16[512,256]{1,0:T(8,128)(2,1)} %latent_attention.1) | data formatting | bytes 524288

commit v3 on v2

--- a/solution.py
+++ b/solution.py
@@ -18,7 +18,7 @@
 SLOTS = 384
 PREFIX = 4096
 QL = 1536
-TB = 512
+TB = 2048
 SCALE2 = math.log2(math.e) / math.sqrt(NOPE + ROPE)
 F32 = jnp.float32
 BF16 = jnp.bfloat16
@@ -241,10 +241,10 @@
 
     live = plen[0]
 
-    def prefix(k, h):
-        yy = yat(k)
+    def prefix(ks, h):
         hc = slice(h * 128, (h + 1) * 128)
-        q = qb[yy].reshape(NZ * RQ, 384)
+        q = jnp.concatenate([qb[yat(k)].reshape(NZ * RQ, 384) for k in ks], axis=0)
+        n = q.shape[0]
         qn = q[:, hc]
         qr = q[:, 256 + h * ROPE : 256 + (h + 1) * ROPE]
 
@@ -258,7 +258,7 @@
                 m = jnp.maximum(m, s[:, j * 128 : (j + 1) * 128])
             return m
 
-        m = lax.fori_loop(0, PREFIX // TB, score, jnp.full((128, 128), -jnp.inf, F32))
+        m = lax.fori_loop(0, PREFIX // TB, score, jnp.full((n, 128), -jnp.inf, F32))
         top = jnp.max(m, axis=1, keepdims=True)
 
         def weigh(t, carry):
@@ -269,22 +269,24 @@
                 den = den + p[:, j * 128 : (j + 1) * 128]
             return acc + nn(p.astype(BF16), vals[pl.ds(t0, TB), hc]), den
 
-        zero = jnp.zeros((128, 128), F32)
+        zero = jnp.zeros((n, 128), F32)
         acc, den = lax.fori_loop(0, PREFIX // TB, weigh, (zero, zero))
         den = jnp.sum(den, axis=1, keepdims=True)
-        po[h, yy] = (acc / den).reshape(NZ, RQ, VD)
-        lse2 = jnp.broadcast_to(top + jnp.log(den) * math.log2(math.e), (128, 128))
-        plse[h, yy] = lse2.reshape(NZ, RQ, 128)
+        mean = acc / den
+        lse2 = jnp.broadcast_to(top + jnp.log(den) * math.log2(math.e), (n, 128))
+        for i, k in enumerate(ks):
+            part = slice(i * 128, (i + 1) * 128)
+            po[h, yat(k)] = mean[part].reshape(NZ, RQ, VD)
+            plse[h, yat(k)] = lse2[part].reshape(NZ, RQ, 128)
 
     loads[4].wait()
     loads[5].wait()
     loads[6].wait()
-    prefix(0, 0)
+    prefix((0, 1), 0)
 
     each(0, NZ, lambda k: landed(ag.at[yat(2), zat(-k)], f_s.at[k], f_r.at[k]))
     queries(2)
 
-    prefix(0, 1)
 
     def arrive(k):
         each(1, NZ, lambda j: landed(zq.at[zat(-j), yat(k)], qz_s.at[k, j], qz_r.at[k, j]))
@@ -343,8 +345,8 @@
     spread_rotary(0, rps.at[y])
     spread(0, 0, absb.at[0, y])
     spread(1, 0, absb.at[1, y])
-    prefix(1, 0)
-    prefix(1, 1)
+    prefix((0, 1), 1)
+    prefix((3, 2), 0)
 
     def wv_landed(k):
         rows = pl.ds(pl.multiple_of(lax.rem(x - k + NX, NX) * 128, 128), 128)
@@ -403,7 +405,7 @@
 
     attend(0)
     attend(1)
-    prefix(3, 0)
+    prefix((3, 2), 1)
     landed(wv.at[:, 1 - c], vc_s.at[0], vc_r.at[0])
     mbuf[...] = jnp.zeros_like(mbuf)
 
@@ -440,10 +442,7 @@
         project(z, recz)
 
     deliver(0)
-    prefix(3, 1)
     deliver(1)
-    prefix(2, 0)
-    prefix(2, 1)
 
     def merge(t, zz, h):
         diag = (
@@ -535,7 +534,7 @@
         vm((2, NZ, 2, NY * RH, VD), BF16),
         vm((2, NZ, 8, 128), F32),
         vm((NZ, 2, NY, RH, VD), F32),
-        vm((128, PREFIX), F32),
+        vm((256, PREFIX), F32),
         vm((2, NY, NZ, RQ, VD), F32),
         vm((2, NY, NZ, RQ, 128), F32),
         dma((8,)),

time: 84.2 us -> 76 us (0.903)
  Pallas kernels: 81.7 us -> 73.5 us
    pallas_call x1, Pallas kernels: 81.7 us -> 73.5 us  [body(): pl.pallas_call(kernel, out_shape=jax.ShapeDtypeStruct((512, 256), BF16),...]
where the time goes in v3:
time: 76 us; the launch traced here: 75.9 us
  Pallas kernels  73.5 us (97%)
  local copies, waits for them, and re-layouts  1.67 us (2%)
    pallas_call x1, Pallas kernels, body(): pl.pallas_call(kernel, out_shape=jax.ShapeDtypeStruct((512, 256), BF16),...  73.5 us
    unnamed x1, local copies, waits for them, and re-layouts  1.67 us

profile of v3, /device:TPU:6, one launch (start us, length us, event | category | flops | bytes accessed | tf_op | source)
XLA Modules:
  0.0 75.9 jit_solution(7909971480421397478)
XLA Ops:
  0.7 73.5 %latent_attention.1 = bf16[512,256]{1,0:T(8,128)(2,1)} custom-call(bf16[16,1536]{1,0:T(8,128)(2,1)} %ql.1, bf16[1536,384]{1,0:T(8,128)(2,1)} %wuq.1, bf16[256,512]{1,0:T(8,128)(2,1)} %wkup.1, bf16[512,256]{1,0:T(8,128)(2,1)} %wvup.1, bf16[4096,256]{1,0:T(8,128)(2,1)} %keys_h.1, bf16[4096,256]{1,0:T(8,128)(2,1)} %vals_h.1, bf16[64,4096]{1,0:T(8,128)(2,1)} %rope_h.1, ...), custom_call_target="tpu_custom_call" | custom-call | flops 5000000000 | bytes 14000000 | tf_op jit(solution)/shard_map/latent_attention/pallas_call | solution.py:545
  74.2 1.7 %copy.13 = bf16[512,256]{1,0:T(8,128)(2,1)} copy(bf16[512,256]{1,0:T(8,128)(2,1)} %latent_attention.1) | data formatting | bytes 524288
